TPU v7x, 256 devices: a whole 4x4x8 slice. The times are simulated.
256 devices in a mesh: tm: 16 (over z, core), row: 16 (over x, y).
Axes of the slice: x: 4, y: 4, z: 8, core: 2. Of those that a mesh axis runs over, the one named last changes fastest.
Arguments:
- hidden_state: bfloat16 [2, 48, 16, 160, 512], P(None, 'tm', 'row'), may hold values from -64 to 64
- grad_out: bfloat16 [2, 48, 16, 160, 512], P(None, 'tm', 'row'), may hold values from -6 to 6
- norm_gain: float32 [512], replicated, may hold values from 0.1 to 1.9
- norm_shift: float32 [512], replicated, may hold values from -4 to 4
- conv_weight: bfloat16 [512, 27, 512], P('row'), may hold values from -0.0546875 to 0.0546875
Outputs:
- grad_hidden: bfloat16 [2, 48, 16, 160, 512], P(None, 'tm', 'row')
All inputs are finite; a program needn't handle non-finite values.
Results may differ from a plain program's by a relative error of at most 0.001.
Values may be sent and summed in bfloat16 or wider, within the bound.
A program may use at most 192 MiB of HBM per device.

v0:
```python
import jax
import jax.numpy as jnp
from jax import lax
from jax.sharding import PartitionSpec as P

GROUPS = 32


def passed_along(value, axis, steps):
    count = lax.axis_size(axis)
    leading, last = (max(0, -steps), min(count, count - steps))
    return lax.ppermute(value, axis, [(source, source + steps) for source in range(leading, last)])


def padded_2(block, sides, width):
    for axis, dim in sides:
        count = lax.axis_size(axis)
        forward = [(i, i + 1) for i in range(count - 1)]
        backward = [(target, source) for source, target in forward]
        low = lax.ppermute(
            lax.slice_in_dim(block, block.shape[dim] - width, None, axis=dim), axis, forward
        )
        high = lax.ppermute(lax.slice_in_dim(block, 0, width, axis=dim), axis, backward)
        block = jnp.concatenate([low, block, high], axis=dim)
    return block


def shards(hidden_state, grad_out, norm_gain, norm_shift, conv_weight):
    hidden_f = hidden_state.astype(jnp.float32)
    clips, frames, rows, width, chan = hidden_f.shape
    per = chan // GROUPS
    count = frames * lax.axis_size("tm") * rows * lax.axis_size("row") * width * per

    def group_sum(value):
        return jnp.sum(value, axis=(1, 2, 3)).reshape(clips, GROUPS, per).sum(-1)

    def spread(stat):
        return jnp.repeat(stat, per, axis=1)[:, None, None, None, :]

    mean = lax.psum(group_sum(hidden_f), ("tm", "row")) / count
    centered = hidden_f - spread(mean)
    variance = lax.psum(group_sum(centered * centered), ("tm", "row")) / count
    rstd = lax.rsqrt(variance + 1e-06)
    normed = centered * spread(rstd)
    pre = normed * norm_gain + norm_shift
    following = passed_along(grad_out[:, :2], "tm", -1)
    extended = jnp.concatenate([grad_out, following], axis=1)
    rimmed = padded_2(extended, (("row", 2),), 1)
    padded = jnp.pad(rimmed, ((0, 0), (0, 0), (0, 0), (1, 1), (0, 0)))
    full_kernel = lax.all_gather(conv_weight, "row", axis=0, tiled=True)
    total = jnp.zeros((clips, frames, rows, width, full_kernel.shape[0]), jnp.float32)
    for kt in range(3):
        for kr in range(3):
            for kw in range(3):
                window = padded[
                    :, 2 - kt : 2 - kt + frames, 2 - kr : 2 - kr + rows, 2 - kw : 2 - kw + width, :
                ]
                total = total + jnp.einsum(
                    "bfrwo,io->bfrwi",
                    window,
                    full_kernel[:, 9 * kt + 3 * kr + kw, :],
                    preferred_element_type=jnp.float32,
                )
    sig = jax.nn.sigmoid(pre)
    slope = sig * (1.0 + pre * (1.0 - sig))
    grad_pre = total * slope * norm_gain
    first_sum, second_sum = lax.psum(
        (group_sum(grad_pre), group_sum(grad_pre * normed)), ("tm", "row")
    )
    first = first_sum / count
    second = second_sum / count
    grad_hidden = spread(rstd) * (grad_pre - spread(first) - normed * spread(second))
    return grad_hidden.astype(jnp.bfloat16)


def solution(mesh):
    return jax.shard_map(
        shards,
        mesh=mesh,
        in_specs=(
            P(None, "tm", "row", None, None),
            P(None, "tm", "row", None, None),
            P(),
            P(),
            P("row", None, None),
        ),
        out_specs=P(None, "tm", "row", None, None),
        check_vma=False,
    )
```

profile of v0, /device:TPU:1, one launch (start us, length us, event | category | flops | bytes accessed | tf_op | source)
XLA Modules:
  0.0 390.0 jit_solution(3871283386164522698)
XLA Ops:
  6.5 0.0 all-gather.2.cloned.1.call-start
  6.5 0.7 all-gather.2.cloned.1.call-update
  7.3 1.1 slice.235
  8.4 0.0 copy-start
  8.4 5.3 %collective-permute-start = (bf16[2,2,1,160,512]{4,3,1,0,2:T(8,128)(2,1)S(1)}, bf16[2,2,1,160,512]{4,3,1,0,2:T(8,128)(2,1)S(1)}, u32[]{:S(2)}, u32[]{:S(2)}) collective-permute-start(bf16[2,2,1,160,512]{4,3,1,0,2:T(8,128)(2,1)S(1)} %slice.235), channel_id=1, source_target_pairs={{16,0},{32,16},{48,32},{64,48},{80,64},{96,80},{112,96},{128,112},... | collective-permute-start | bytes 1966088 | tf_op jit(solution)/shard_map/ppermute | solution.py:12
  13.7 8.0 %collective-permute-done = bf16[2,2,1,160,512]{4,3,1,0,2:T(8,128)(2,1)S(1)} collective-permute-done((bf16[2,2,1,160,512]{4,3,1,0,2:T(8,128)(2,1)S(1)}, bf16[2,2,1,160,512]{4,3,1,0,2:T(8,128)(2,1)S(1)}, u32[]{:S(2)}, u32[]{:S(2)}) %collective-permute-start) | collective-permute-done | bytes 655392 | tf_op jit(solution)/shard_map/ppermute | solution.py:12
  21.7 1.3 pad_maximum_fusion
  23.0 1.3 collective-permute-start.2
  24.3 5.5 %collective-permute-start.1 = (bf16[2,5,1,160,512]{4,3,1,0,2:T(8,128)(2,1)}, bf16[2,5,1,160,512]{4,3,1,0,2:T(8,128)(2,1)}, u32[]{:S(2)}, u32[]{:S(2)}) collective-permute-start(bf16[2,5,1,160,512]{4,3,1,0,2:T(8,128)(2,1)} %pad_maximum_fusion), channel_id=1, source_target_pairs={{0,1},{1,2},{2,3},{3,4},{4,5},{5,6},{6,7},{7,8},{8,9},{9,10},{10,1... | collective-permute-start | bytes 4915208 | tf_op jit(solution)/shard_map/ppermute | solution.py:20
  29.8 0.0 copy-done
  29.8 0.2 convert_reduce_fusion
  30.0 0.1 reshape.164
  30.1 0.1 reduce_sum.73
  30.1 117.8 %psum.28 = f32[2,32]{1,0:T(2,128)S(1)} all-reduce(f32[2,32]{1,0:T(2,128)S(1)} %reduce_sum.73), channel_id=1, replica_groups=mesh['tm'=16,'row'=16] {'tm','row'}, use_global_device_ids=true, to_apply=%region_2.0 | all-reduce | flops 64 | bytes 512 | tf_op jit(solution)/shard_map/psum | solution.py:40
  147.9 0.1 broadcast_in_dim.16
  148.0 0.1 sub.26
  148.1 0.3 fusion.23
  148.4 0.1 reshape.165
  148.5 0.1 reduce_sum.75
  148.5 72.4 %psum.29 = f32[2,32]{1,0:T(2,128)S(1)} all-reduce(f32[2,32]{1,0:T(2,128)S(1)} %reduce_sum.75), channel_id=1, replica_groups=mesh['tm'=16,'row'=16] {'tm','row'}, use_global_device_ids=true, to_apply=%region_5.0 | all-reduce | flops 64 | bytes 512 | tf_op jit(solution)/shard_map/psum | solution.py:42
  221.0 0.1 broadcast_in_dim.17
  221.0 0.1 mul.56
  221.1 0.0 collective-permute-done.2
  221.2 0.0 collective-permute-done.1
  221.2 6.8 %select_maximum_fusion = bf16[2,5,3,162,512]{4,3,1,0,2:T(8,128)(2,1)} fusion(bf16[2,5,1,160,512]{4,3,1,0,2:T(8,128)(2,1)} %collective-permute-done.2, bf16[2,5,1,160,512]{4,3,1,0,2:T(8,128)(2,1)} %collective-permute-done.1, bf16[2,2,1,160,512]{4,3,1,0,2:T(8,128)(2,1)S(1)} %collective-permute-done, bf16[2,3,1,160,512]{4,3,1,0,2:T(8,128)(2,1)S(1)} %bitcast.292), kind=kLoop, calls=%fused_computation.3 | loop fusion | flops 37324800 | bytes 9891840 | tf_op jit(solution)/shard_map/concatenate | solution.py:24
  227.9 3.5 fusion.34
  231.4 4.1 %fusion.42 = f32[2,3,160,512]{3,2,1,0:T(8,128)} fusion(bf16[2,5,1,160,512]{4,3,1,0,2:T(8,128)(2,1)} %collective-permute-done.1, bf16[512,27,512]{2,0,1:T(8,128)(2,1)} %all-gather.2.cloned.1.call-done), kind=kOutput, calls=%fused_computation.61 | convolution fusion | flops 503316480 | bytes 3473408 | tf_op jit(solution)/shard_map/bfrwo,io->bfrwi/dot_general | solution.py:58
  235.5 3.4 fusion.50
  238.9 3.5 fusion.39
  242.4 3.3 fusion.47
  245.7 3.2 fusion.55
  248.9 0.0 slice-done.1
  248.9 2.0 fusion.35
  250.9 2.0 fusion.36
  252.9 2.0 fusion.37
  254.9 2.0 fusion.38
  256.9 2.0 fusion.40
  258.9 2.0 fusion.41
  260.9 2.0 fusion.43
  263.0 2.0 fusion.44
  265.0 2.0 fusion.45
  267.0 2.1 fusion.46
  269.0 2.0 fusion.48
  271.0 2.0 fusion.49
  273.0 2.0 fusion.51
  275.0 1.9 fusion.52
  276.9 2.0 fusion.53
  278.9 2.0 fusion.54
  280.9 2.0 fusion.56
  282.9 2.2 fusion.26
  285.2 2.0 fusion.30
  287.2 2.0 fusion.57
  289.1 0.0 copy-done.3
  289.1 17.8 %fusion.61 = (f32[2,512]{1,0:T(2,128)S(1)}, f32[2,512]{1,0:T(2,128)S(1)}, f32[2,3,1,160,512]{4,3,1,0,2:T(8,128)S(1)}) fusion(f32[2,512]{1,0:T(2,128)S(1)} %mul.56, f32[2,512]{1,0:T(2,128)S(1)} %sub.26, bf16[2,3,1,160,512]{4,3,2,1,0:T(8,128)(2,1)S(1)} %copy-done, f32[512]{0:T(512)S(1)} %copy-done.3, f32[512]{0:T(512)S(1)} %copy-done.4, ...), kind=kOutput, calls=%fused_computation.125 | convolution fusion | flops 524449792 | bytes 55595008 | tf_op jit(solution)/shard_map/bfrwo,io->bfrwi/dot_general | solution.py:58
  307.0 0.1 reshape.193
  307.1 0.1 reduce_sum.77
  307.2 0.1 reshape.194
  307.2 0.1 reduce_sum.79
  307.3 74.1 %all-reduce.1 = (f32[2,32]{1,0:T(2,128)S(1)}, f32[2,32]{1,0:T(2,128)S(1)}) all-reduce(f32[2,32]{1,0:T(2,128)S(1)} %reduce_sum.79, f32[2,32]{1,0:T(2,128)S(1)} %reduce_sum.77), channel_id=1, replica_groups=mesh['tm'=16,'row'=16] {'tm','row'}, use_global_device_ids=true, to_apply=%region_11.12 | all-reduce | flops 128 | bytes 1024 | tf_op jit(solution)/shard_map/psum | solution.py:67
  381.4 0.1 broadcast_in_dim.19
  381.5 0.1 mul.66
  381.6 0.1 broadcast_in_dim.18
  381.7 0.1 sub.30
  381.8 1.4 fusion.32
  (15 shorter events, 0.0 us)
Async XLA Ops:
  6.5 15.2 %copy-start.1 = (bf16[2,3,1,160,512]{4,3,2,1,0:T(8,128)(2,1)S(1)}, bf16[2,3,1,160,512]{4,3,2,1,0:T(8,128)(2,1)}, u32[]{:S(2)}) copy-start(bf16[2,3,1,160,512]{4,3,2,1,0:T(8,128)(2,1)} %param.6) | copy-start | bytes 2949124
  6.5 221.4 %all-gather.2.cloned.1.call-start = ((), (), s32[]{:S(2)}) async-start(), calls=%async_computation | async-start | bytes 15040512 | tf_op jit(solution)/shard_map/all_gather | solution.py:50
  8.4 21.4 %copy-start = (bf16[2,3,1,160,512]{4,3,2,1,0:T(8,128)(2,1)S(1)}, bf16[2,3,1,160,512]{4,3,2,1,0:T(8,128)(2,1)}, u32[]{:S(2)}) copy-start(bf16[2,3,1,160,512]{4,3,2,1,0:T(8,128)(2,1)} %param.5) | copy-start | bytes 2949124
  8.4 13.3 %collective-permute-start = (bf16[2,2,1,160,512]{4,3,1,0,2:T(8,128)(2,1)S(1)}, bf16[2,2,1,160,512]{4,3,1,0,2:T(8,128)(2,1)S(1)}, u32[]{:S(2)}, u32[]{:S(2)}) collective-permute-start(bf16[2,2,1,160,512]{4,3,1,0,2:T(8,128)(2,1)S(1)} %slice.235), channel_id=1, source_target_pairs={{16,0},{32,16},{48,32},{64,48},{80,64},{96,80},{112,96},{128,112},... | collective-permute-start | bytes 1966088 | tf_op jit(solution)/shard_map/ppermute | solution.py:12
  23.0 198.1 %collective-permute-start.2 = (bf16[2,5,1,160,512]{4,3,1,0,2:T(8,128)(2,1)}, bf16[2,5,1,160,512]{4,3,1,0,2:T(8,128)(2,1)}, u32[]{:S(2)}, u32[]{:S(2)}) collective-permute-start(bf16[2,5,1,160,512]{4,3,1,0,2:T(8,128)(2,1)} %pad_maximum_fusion), channel_id=1, source_target_pairs={{1,0},{2,1},{3,2},{4,3},{5,4},{6,5},{7,6},{8,7},{9,8},{10,9},{11,1... | collective-permute-start | bytes 4915208 | tf_op jit(solution)/shard_map/ppermute | solution.py:23
  24.3 196.8 %collective-permute-start.1 = (bf16[2,5,1,160,512]{4,3,1,0,2:T(8,128)(2,1)}, bf16[2,5,1,160,512]{4,3,1,0,2:T(8,128)(2,1)}, u32[]{:S(2)}, u32[]{:S(2)}) collective-permute-start(bf16[2,5,1,160,512]{4,3,1,0,2:T(8,128)(2,1)} %pad_maximum_fusion), channel_id=1, source_target_pairs={{0,1},{1,2},{2,3},{3,4},{4,5},{5,6},{6,7},{7,8},{8,9},{9,10},{10,1... | collective-permute-start | bytes 4915208 | tf_op jit(solution)/shard_map/ppermute | solution.py:20
  227.9 17.7 %copy-start.2 = (bf16[512,27,512]{2,0,1:T(8,128)(2,1)S(1)}, bf16[512,27,512]{2,0,1:T(8,128)(2,1)}, u32[]{:S(2)}) copy-start(bf16[512,27,512]{2,0,1:T(8,128)(2,1)} %all-gather.2.cloned.1.call-done) | copy-start | bytes 42467332
  231.4 17.5 %slice-start = ((s8[5160960]{0:T(1024)(128)(4,1)}), s8[4194304]{0:T(1024)(128)(4,1)S(1)}, s32[]{:S(2)}) async-start(s8[5160960]{0:T(1024)(128)(4,1)} %bitcast.288), calls=%async_computation.1 | async-start | bytes 8388608
  238.9 10.0 %slice-start.1 = ((s8[5160960]{0:T(1024)(128)(4,1)}), s8[966656]{0:T(1024)(128)(4,1)S(1)}, s32[]{:S(2)}) async-start(s8[5160960]{0:T(1024)(128)(4,1)} %bitcast.288), calls=%async_computation.2 | async-start | bytes 1933312
  287.2 2.0 copy-start.3
  287.2 2.0 copy-start.4
Sparse Core Ops, SparseCore 0:
  9.8 141.7 all-gather.1
where the time goes:
time: 391 us; the launch traced here: 390 us
  blocking collectives  264 us (68%)
  matrix products  79 us (20%)
  between operations  13.5 us (3%)
  starting transfers between devices  12 us (3%)
  other arithmetic  10.3 us (3%)
  waiting for transfers between devices  8.76 us (2%)
    psum x1, blocking collectives, shards(): mean = lax.psum(group_sum(hidden_f), ('tm', 'row')) / count  118 us
    dot_general x27, matrix products, shards(): jnp.einsum('bfrwo,io->bfrwi', window, full_kernel[:, 9 * kt + 3 * kr + kw...  79 us
    psum x1, blocking collectives, shards(): lax.psum((group_sum(grad_pre), group_sum(grad_pre * normed)), ('tm', 'row'))  74.1 us
    psum x1, blocking collectives, shards(): variance = lax.psum(group_sum(centered * centered), ('tm', 'row')) / count  72.4 us
    ppermute x1, waiting for transfers between devices, passed_along(): lax.ppermute(value, axis, [(source, source + steps) for source in range(l...  8.04 us
  transfers between devices with their start and end apart: 4, of which 1 were waited for; matrix products, arithmetic and copies ran while one was open for 3% of the time, Pallas kernels for 0%

commit v1 on v0

v1 whole, which is shorter than its diff:
```python
import functools

import jax
import jax.numpy as jnp
from jax import lax
from jax.experimental import pallas as pl
from jax.experimental.pallas import tpu as pltpu
from jax.sharding import PartitionSpec as P

GROUPS = 32
MESH = pl.DeviceIdType.MESH
F32 = jnp.float32
ORDER = (3, 5, 4, 0, 2, 1, 6, 8, 7)
Y_FIRST = (True, True, False, True, True, False, True, True, True)
CHUNKS = 9
EPS = 1e-06


def group_total(value, per):
    lane = lax.broadcasted_iota(jnp.int32, value.shape, 1)
    size = value.shape[1]
    step = 1
    while step < per:
        other = jnp.where(
            (lane & step) != 0, pltpu.roll(value, step, 1), pltpu.roll(value, size - step, 1)
        )
        value = value + other
        step *= 2
    return value


def kernel(
    count,
    hid_hbm, cot_hbm, gain_ref, shift_ref, wt_hbm, out_hbm,
    kern, cot, acc, hid, normed, scale, result, local, gathered, moments,
    w_send, w_recv, h_send, h_recv, f_send, f_recv, c_send, c_recv,
    x_send, x_recv, load_sem, out_sem,
):
    tm, row = lax.axis_index("tm"), lax.axis_index("row")
    core = lax.rem(tm, 2)
    px, py = row // 4, lax.rem(row, 4)
    way = 1 - 2 * core
    per = gain_ref.shape[1] // GROUPS
    local_count = 3 * 160 * per

    def wrap(value, size):
        return lax.rem(value + size, size)

    def at_row(value):
        return (tm, wrap(value, 16))

    def at_tm(value):
        return (wrap(value, 16), row)

    def at_xy(x, y):
        return (tm, wrap(x, 4) * 4 + wrap(y, 4))

    partner = (tm + way, row)

    def remote(src, dst, send, recv, target):
        return pltpu.make_async_remote_copy(
            src_ref=src, dst_ref=dst, send_sem=send, recv_sem=recv,
            device_id=target, device_id_type=MESH,
        )

    def along(k, step):
        return at_xy(px, py + step) if Y_FIRST[k] else at_xy(px + step, py)

    def across(k, step):
        return at_xy(px + step, py) if Y_FIRST[k] else at_xy(px, py + step)

    def piece(k, step, half):
        x, y = (px, wrap(py + step, 4)) if Y_FIRST[k] else (wrap(px + step, 4), py)
        return kern.at[:, ORDER[k], x, y, half]

    def block(k, step, half):
        if Y_FIRST[k]:
            return kern.at[:, ORDER[k], wrap(px + step, 4), :, half]
        return kern.at[:, ORDER[k], :, wrap(py + step, 4), half]

    def first_copy(k, slot):
        step = (1, -1, 2)[slot]
        return remote(
            wt_hbm.at[:, ORDER[k], core], piece(k, 0, core),
            w_send.at[k, slot], w_recv.at[k, slot], along(k, step),
        )

    def first_arrival(k, slot):
        step = (1, -1, 2)[slot]
        mine = piece(k, -step, core)
        return remote(mine, mine, w_send.at[k, slot], w_recv.at[k, slot], along(k, step))

    def second_copy(k, slot):
        step = (1, -1)[slot]
        mine = block(k, 0, core)
        return remote(mine, mine, w_send.at[k, 3 + slot], w_recv.at[k, 3 + slot], across(k, step))

    def second_arrival(k, slot):
        step = (1, -1)[slot]
        mine = block(k, -step, core)
        return remote(mine, mine, w_send.at[k, 3 + slot], w_recv.at[k, 3 + slot], across(k, step))

    def onward_copy(k):
        mine = block(k, -way, core)
        return remote(mine, mine, w_send.at[k, 5], w_recv.at[k, 5], across(k, way))

    def onward_arrival(k):
        mine = block(k, 2, core)
        return remote(mine, mine, w_send.at[k, 5], w_recv.at[k, 5], across(k, way))

    def core_copy(k, slot, half):
        mine = block(k, (0, -1, 1, 2)[slot], half)
        return remote(mine, mine, w_send.at[k, 6 + slot], w_recv.at[k, 6 + slot], partner)

    def stage_1(k):
        for slot in (2, 0, 1):
            first_copy(k, slot).start()

    def stage_2(k):
        for slot in range(3):
            first_arrival(k, slot).wait_recv()
        for slot in range(2):
            second_copy(k, slot).start()
        core_copy(k, 0, core).start()

    def stage_3(k):
        for slot in range(2):
            second_arrival(k, slot).wait_recv()
        onward_copy(k).start()
        for slot in range(2):
            core_copy(k, 1 + slot, core).start()

    def stage_4(k):
        onward_arrival(k).wait_recv()
        core_copy(k, 3, core).start()

    def settle(k):
        for slot in range(4):
            core_copy(k, slot, 1 - core).wait_recv()

    def row_copy(side, f, b):
        step = (1, -1)[side]
        return remote(
            cot_hbm.at[b, f, 0], cot.at[2 * side, 2 * f + b],
            h_send.at[side, 2 * f + b], h_recv.at[side, 2 * f + b], at_row(row + step),
        )

    def frame_copy(f, b):
        return remote(
            cot_hbm.at[b, f, 0], cot.at[1, 6 + 2 * f + b],
            f_send.at[2 * f + b], f_recv.at[2 * f + b], at_tm(tm - 1),
        )

    def corner_copy(side):
        return remote(
            cot.at[2 * side, pl.ds(0, 4)], cot.at[2 * side, pl.ds(6, 4)],
            c_send.at[side], c_recv.at[side], at_tm(tm - 1),
        )

    def start_rows(side):
        for f in range(3):
            for b in range(2):
                row_copy(side, f, b).start()

    def finish_rows(side):
        for f in range(3):
            for b in range(2):
                row_copy(side, f, b).wait_recv()

        @pl.when(row == (0, 15)[side])
        def _():
            cot[2 * side, pl.ds(0, 6)] = jnp.zeros((6, 160, 512), cot.dtype)

        corner_copy(side).start()

    def finish_corner(side):
        corner_copy(side).wait_recv()

        @pl.when(tm == 15)
        def _():
            cot[2 * side, pl.ds(6, 4)] = jnp.zeros((4, 160, 512), cot.dtype)

    def finish_frames():
        for f in range(2):
            for b in range(2):
                frame_copy(f, b).wait_recv()

        @pl.when(tm == 15)
        def _():
            cot[1, pl.ds(6, 4)] = jnp.zeros((4, 160, 512), cot.dtype)

    def exchange_copy(e, k):
        if e % 2 == 0:
            me, target = row, at_row(row + k)
        else:
            me, target = tm, at_tm(tm + k)
        return remote(local.at[e], gathered.at[e, me], x_send.at[e, k], x_recv.at[e, me], target)

    def exchange_start(e):
        me = row if e % 2 == 0 else tm
        gathered[e, me] = local[e]

        def body(k, carry):
            exchange_copy(e, k).start()
            return carry

        lax.fori_loop(1, 16, body, 0)

    def exchange_finish(e):
        me = row if e % 2 == 0 else tm

        def body(k, carry):
            other = lax.rem(me + k, 16)
            there = gathered.at[e, other]
            remote(there, there, x_send.at[e, k], x_recv.at[e, other], partner).wait_recv()
            return carry

        lax.fori_loop(1, 16, body, 0)

    def merge(e, each):
        stats = [gathered[e, i] for i in range(16)]
        mean = functools.reduce(jnp.add, [s[0:2] for s in stats]) * (1.0 / 16)
        square = functools.reduce(jnp.add, [s[2:4] for s in stats])
        for s in stats:
            apart = s[0:2] - mean
            square = square + each * (apart * apart)
        return mean, square

    def matmul_chunk(k):
        j = ORDER[k]
        kr, kw = j // 3, j % 3

        def body(m, carry):
            total = None
            for kt in range(3):
                lhs = cot[2 - kr, pl.ds(2 * (2 - kt) + 3 * m, 3)].reshape(480, 512)
                rhs = kern[kt, j].reshape(512, 512)
                part = lax.dot_general(
                    lhs, rhs, (((1,), (1,)), ((), ())), preferred_element_type=F32
                )
                total = part if total is None else total + part
            total = total.reshape(3, 160, 512)
            here = pl.ds(3 * m, 3)
            if k < 3:
                acc[kw, here] = total
            else:
                acc[kw, here] = acc[kw, here] + total
            return carry

        lax.fori_loop(0, 2, body, 0)

    def fold_columns():
        def body(s, carry):
            place = lax.broadcasted_iota(jnp.int32, (160, 512), 0)
            later = jnp.where(place < 159, pltpu.roll(acc[0, s], 159, 0), 0.0)
            earlier = jnp.where(place > 0, pltpu.roll(acc[2, s], 1, 0), 0.0)
            acc[1, s] = acc[1, s] + later + earlier
            return carry

        lax.fori_loop(0, 6, body, 0)

    barrier = pltpu.get_barrier_semaphore()

    def greet(k, carry):
        pl.semaphore_signal(barrier, inc=1, device_id=at_row(row + k), device_id_type=MESH)
        pl.semaphore_signal(barrier, inc=1, device_id=at_tm(tm + k), device_id_type=MESH)
        return carry

    lax.fori_loop(1, 16, greet, 0)

    loads = [
        pltpu.make_async_copy(wt_hbm.at[:, :, core], kern.at[:, :, px, py, core], load_sem.at[0])
    ]
    for f in range(3):
        for b in range(2):
            s = 2 * f + b
            loads.append(
                pltpu.make_async_copy(hid_hbm.at[b, f, 0], hid.at[s], load_sem.at[1 + s])
            )
    for f in range(3):
        for b in range(2):
            s = 2 * f + b
            loads.append(
                pltpu.make_async_copy(cot_hbm.at[b, f, 0], cot.at[1, s], load_sem.at[7 + s])
            )
    for load in loads:
        load.start()

    pl.semaphore_wait(barrier, 30)
    stage_1(0)
    stage_1(1)
    for f in range(2):
        for b in range(2):
            frame_copy(f, b).start()
    start_rows(1)
    for load in loads:
        load.wait()

    def add_up(fn):
        rows = []
        for b in range(2):
            total = None
            for f in range(3):
                part = jnp.sum(fn(2 * f + b, b), axis=0, keepdims=True)
                total = part if total is None else total + part
            rows.append(total)
        return jnp.concatenate(rows, axis=0)

    own_mean = group_total(add_up(lambda s, b: hid[s].astype(F32)), per) * (1.0 / local_count)

    def deviation(s, b):
        apart = hid[s].astype(F32) - own_mean[b : b + 1]
        return apart * apart

    own_square = group_total(add_up(deviation), per)
    local[0, 0:2] = own_mean
    local[0, 2:4] = own_square
    local[0, 4:8] = jnp.zeros((4, 512), F32)
    exchange_start(0)

    def merge_rows():
        exchange_finish(0)
        mean, square = merge(0, float(local_count))
        local[1, 0:2] = mean
        local[1, 2:4] = square
        local[1, 4:8] = jnp.zeros((4, 512), F32)
        exchange_start(1)

    def merge_all():
        exchange_finish(1)
        mean, square = merge(1, float(local_count) * 16)
        rstd = lax.rsqrt(square * (1.0 / count) + EPS)
        moments[0:2] = mean
        moments[2:4] = rstd

    def prepare():
        def body(s, carry):
            b = lax.rem(s, 2)
            mean, rstd = moments[pl.ds(b, 1)], moments[pl.ds(2 + b, 1)]
            unit = (hid[s].astype(F32) - mean) * rstd
            pre = unit * gain_ref[...] + shift_ref[...]
            sig = 1.0 / (1.0 + jnp.exp(-pre))
            normed[s] = unit
            scale[s] = sig * (1.0 + pre * (1.0 - sig)) * gain_ref[...]
            return carry

        lax.fori_loop(0, 6, body, 0)

    for t in range(CHUNKS + 3):
        if t < CHUNKS:
            stage_2(t)
        if t + 2 < CHUNKS:
            stage_1(t + 2)
        if t == 0:
            start_rows(0)
        if 0 <= t - 1 < CHUNKS:
            stage_3(t - 1)
        if 0 <= t - 2 < CHUNKS:
            stage_4(t - 2)
        if t == 2:
            merge_rows()
            finish_frames()
        if t == 3:
            finish_rows(1)
        if t == 4:
            merge_all()
            finish_rows(0)
        if t == 5:
            prepare()
        k = t - 3
        if k >= 0:
            if k == 3:
                finish_corner(1)
            if k == 6:
                finish_corner(0)
            settle(k)
            matmul_chunk(k)
            if k == CHUNKS - 2:
                fold_columns()

    def terms(s, b):
        grad = acc[1, s] * scale[s]
        acc[1, s] = grad
        return grad

    first = add_up(terms)
    second = add_up(lambda s, b: acc[1, s] * normed[s])
    local[2, 0:4] = group_total(jnp.concatenate([first, second], axis=0), per)
    local[2, 4:8] = jnp.zeros((4, 512), F32)
    exchange_start(2)
    exchange_finish(2)
    local[3] = functools.reduce(jnp.add, [gathered[2, i] for i in range(16)])
    exchange_start(3)
    exchange_finish(3)
    means = functools.reduce(jnp.add, [gathered[3, i] for i in range(16)]) * (1.0 / count)

    stores = []
    for s in range(6):
        f, b = s // 2, s % 2
        rstd = moments[2 + b : 3 + b]
        value = rstd * (acc[1, s] - means[b : b + 1] - normed[s] * means[2 + b : 3 + b])
        result[s] = value.astype(result.dtype)
        store = pltpu.make_async_copy(result.at[s], out_hbm.at[b, f, 0], out_sem.at[s])
        store.start()
        stores.append(store)

    for k in range(CHUNKS):
        for slot in range(3):
            first_copy(k, slot).wait_send()
        for slot in range(2):
            second_copy(k, slot).wait_send()
        onward_copy(k).wait_send()
        for slot in range(4):
            core_copy(k, slot, core).wait_send()
    for f in range(3):
        for b in range(2):
            for side in range(2):
                row_copy(side, f, b).wait_send()
            if f < 2:
                frame_copy(f, b).wait_send()
    for side in range(2):
        corner_copy(side).wait_send()

    def sent(k, carry):
        for e in range(4):
            exchange_copy(e, k).wait_send()
        return carry

    lax.fori_loop(1, 16, sent, 0)
    for store in stores:
        store.wait()


def shards(hidden_state, grad_out, norm_gain, norm_shift, conv_weight):
    clips, frames, rows, width, chan = hidden_state.shape
    devices = lax.axis_size("tm") * lax.axis_size("row")
    count = clips * frames * rows * width * chan // clips // GROUPS * devices
    taps = jnp.swapaxes(conv_weight, 0, 1).reshape(3, 9, 2, 16, chan)
    bf16 = jnp.bfloat16
    anywhere = pl.BlockSpec(memory_space=pl.ANY)
    vmem = pl.BlockSpec(memory_space=pltpu.VMEM)
    dma = pltpu.SemaphoreType.DMA
    return pl.pallas_call(
        functools.partial(kernel, count),
        out_shape=jax.ShapeDtypeStruct(hidden_state.shape, bf16),
        in_specs=[anywhere, anywhere, vmem, vmem, anywhere],
        out_specs=anywhere,
        scratch_shapes=[
            pltpu.VMEM((3, 9, 4, 4, 2, 16, chan), bf16),
            pltpu.VMEM((3, 10, width, chan), bf16),
            pltpu.VMEM((3, 6, width, chan), F32),
            pltpu.VMEM((6, width, chan), bf16),
            pltpu.VMEM((6, width, chan), F32),
            pltpu.VMEM((6, width, chan), F32),
            pltpu.VMEM((6, width, chan), bf16),
            pltpu.VMEM((4, 8, chan), F32),
            pltpu.VMEM((4, 16, 8, chan), F32),
            pltpu.VMEM((4, chan), F32),
            dma((CHUNKS, 10)), dma((CHUNKS, 10)),
            dma((2, 6)), dma((2, 6)),
            dma((4,)), dma((4,)),
            dma((2,)), dma((2,)),
            dma((4, 16)), dma((4, 16)),
            dma((13,)), dma((6,)),
        ],
        compiler_params=pltpu.CompilerParams(
            collective_id=0, has_side_effects=True, vmem_limit_bytes=56 << 20
        ),
        name="conv_grad",
    )(hidden_state, grad_out, norm_gain.reshape(1, chan), norm_shift.reshape(1, chan), taps)


def solution(mesh):
    return jax.shard_map(
        shards,
        mesh=mesh,
        in_specs=(
            P(None, "tm", "row", None, None),
            P(None, "tm", "row", None, None),
            P(),
            P(),
            P("row", None, None),
        ),
        out_specs=P(None, "tm", "row", None, None),
        check_vma=False,
    )
```

time: 391 us -> 141 us (0.36)
  blocking collectives: 264 us -> 0 us
  Pallas kernels: 0 us -> 139 us
  matrix products: 79 us -> 0 us
  between operations: 13.5 us -> 0.01 us
  starting transfers between devices: 12 us -> 0 us
  other arithmetic: 10.3 us -> 0 us
  waiting for transfers between devices: 8.76 us -> 0 us
    psum x3 -> x0, blocking collectives: 264 us -> none  [the longest x1 118 us: shards(): mean = lax.psum(group_sum(hidden_f), ('tm', 'row')) / count]
    pallas_call x0 -> x1, Pallas kernels: none -> 139 us  [shards(): pl.pallas_call(functools.partial(kernel, count), out_shape=jax.ShapeDtype...]
    dot_general x27 -> x0, matrix products: 79 us -> none  [shards(): jnp.einsum('bfrwo,io->bfrwi', window, full_kernel[:, 9 * kt + 3 * kr + kw...]
    ppermute x3 -> x0, starting transfers between devices: 12 us -> none  [the longest x1 5.47 us: padded_2(): lax.ppermute(lax.slice_in_dim(block, block.shape[dim] - width, None, axis...]
    concatenate x2 -> x0, other arithmetic: 8.07 us -> none  [the longest x1 6.78 us: padded_2(): block = jnp.concatenate([low, block, high], axis=dim)]
    ppermute x3 -> x0, waiting for transfers between devices: 8.05 us -> none  [the longest x1 8.04 us: passed_along(): lax.ppermute(value, axis, [(source, source + steps) for source in range(l...]
  transfers between devices with their start and end apart: 4 -> 0, of which waited for: 1 -> 0; matrix products, arithmetic and copies ran while one was open for 3% -> 0% of each run, Pallas kernels for 0% -> 0%
where the time goes in v1:
time: 141 us
  Pallas kernels  139 us (99%)
  local copies, waits for them, and re-layouts  2.26 us (2%)
    pallas_call x1, Pallas kernels, shards(): pl.pallas_call(functools.partial(kernel, count), out_shape=jax.ShapeDtype...  139 us

profile of v1, /device:TPU:1, one launch (start us, length us, event | category | flops | bytes accessed | tf_op | source)
XLA Modules:
  0.0 141.3 jit_solution(17935117291986590327)
XLA Ops:
  0.0 139.1 %conv_grad.1 = bf16[2,3,1,160,512]{4,3,2,1,0:T(8,128)(2,1)} custom-call(bf16[2,3,1,160,512]{4,3,2,1,0:T(8,128)(2,1)} %hid_hbm.1, bf16[2,3,1,160,512]{4,3,2,1,0:T(8,128)(2,1)} %cot_hbm.1, f32[1,512]{1,0:T(1,128)} %bitcast.6, f32[1,512]{1,0:T(1,128)} %bitcast.7, bf16[3,9,2,16,512]{4,3,2,1,0:T(8,128)(2,1)} %bitcast.5), custom_call_target="tpu_custom_call" | custom-call | tf_op jit(solution)/shard_map/conv_grad/pallas_call | solution.py:443
  139.1 2.3 %copy.7 = bf16[2,3,1,160,512]{4,3,2,1,0:T(8,128)(2,1)} copy(bf16[2,3,1,160,512]{4,3,2,1,0:T(8,128)(2,1)} %conv_grad.1) | data formatting | bytes 1966080

commit v2 on v1

--- a/solution.py
+++ b/solution.py
@@ -10,9 +10,11 @@
 GROUPS = 32
 MESH = pl.DeviceIdType.MESH
 F32 = jnp.float32
-ORDER = (3, 5, 4, 0, 2, 1, 6, 8, 7)
-Y_FIRST = (True, True, False, True, True, False, True, True, True)
-CHUNKS = 9
+ITEMS = (
+    (1, True, True), (1, False, True), (0, True, True),
+    (2, True, True), (0, False, True), (2, False, False),
+)
+SHARED = tuple(i for i, item in enumerate(ITEMS) if item[1])
 EPS = 1e-06
 
 
@@ -33,13 +35,14 @@
     count,
     hid_hbm, cot_hbm, gain_ref, shift_ref, wt_hbm, out_hbm,
     kern, cot, acc, hid, normed, scale, result, local, gathered, moments,
-    w_send, w_recv, h_send, h_recv, f_send, f_recv, c_send, c_recv,
+    w_send, w_recv, z_send, z_recv, h_send, h_recv, f_send, f_recv, c_send, c_recv,
     x_send, x_recv, load_sem, out_sem,
 ):
     tm, row = lax.axis_index("tm"), lax.axis_index("row")
     core = lax.rem(tm, 2)
     px, py = row // 4, lax.rem(row, 4)
     way = 1 - 2 * core
+    odd = lax.rem(tm // 2, 2)
     per = gain_ref.shape[1] // GROUPS
     local_count = 3 * 160 * per
 
@@ -63,25 +66,32 @@
             device_id=target, device_id_type=MESH,
         )
 
+    def tap(k):
+        return 3 * ITEMS[k][0] + (2 * odd if ITEMS[k][1] else 1)
+
+    def other_tap(n):
+        return 3 * ITEMS[SHARED[n]][0] + 2 - 2 * odd
+
     def along(k, step):
-        return at_xy(px, py + step) if Y_FIRST[k] else at_xy(px + step, py)
+        return at_xy(px, py + step) if ITEMS[k][2] else at_xy(px + step, py)
 
     def across(k, step):
-        return at_xy(px + step, py) if Y_FIRST[k] else at_xy(px, py + step)
+        return at_xy(px + step, py) if ITEMS[k][2] else at_xy(px, py + step)
 
     def piece(k, step, half):
-        x, y = (px, wrap(py + step, 4)) if Y_FIRST[k] else (wrap(px + step, 4), py)
-        return kern.at[:, ORDER[k], x, y, half]
-
-    def block(k, step, half):
-        if Y_FIRST[k]:
-            return kern.at[:, ORDER[k], wrap(px + step, 4), :, half]
-        return kern.at[:, ORDER[k], :, wrap(py + step, 4), half]
+        x, y = (px, wrap(py + step, 4)) if ITEMS[k][2] else (wrap(px + step, 4), py)
+        return kern.at[:, tap(k), x, y, half]
+
+    def block(k, step, half, chosen=None):
+        chosen = tap(k) if chosen is None else chosen
+        if ITEMS[k][2]:
+            return kern.at[:, chosen, wrap(px + step, 4), :, half]
+        return kern.at[:, chosen, :, wrap(py + step, 4), half]
 
     def first_copy(k, slot):
         step = (1, -1, 2)[slot]
         return remote(
-            wt_hbm.at[:, ORDER[k], core], piece(k, 0, core),
+            wt_hbm.at[:, tap(k), core], piece(k, 0, core),
             w_send.at[k, slot], w_recv.at[k, slot], along(k, step),
         )
 
@@ -108,35 +118,64 @@
         mine = block(k, 2, core)
         return remote(mine, mine, w_send.at[k, 5], w_recv.at[k, 5], across(k, way))
 
+    STEPS = (0, -1, 1, 2)
+
     def core_copy(k, slot, half):
-        mine = block(k, (0, -1, 1, 2)[slot], half)
+        mine = block(k, STEPS[slot], half)
         return remote(mine, mine, w_send.at[k, 6 + slot], w_recv.at[k, 6 + slot], partner)
+
+    def plane_copy(n, slot):
+        mine = block(SHARED[n], STEPS[slot], core)
+        step = 1 if n == 0 else way
+        return remote(mine, mine, z_send.at[n, slot], z_recv.at[n, slot], at_tm(tm + 2 * step))
+
+    def plane_arrival(n, slot):
+        mine = block(SHARED[n], STEPS[slot], core, other_tap(n))
+        return remote(mine, mine, z_send.at[n, slot], z_recv.at[n, slot], partner)
+
+    def pass_copy(n, slot, half):
+        mine = block(SHARED[n], STEPS[slot], half, other_tap(n))
+        return remote(mine, mine, z_send.at[n, 4 + slot], z_recv.at[n, 4 + slot], partner)
 
     def stage_1(k):
         for slot in (2, 0, 1):
             first_copy(k, slot).start()
+
+    def hand_on(k, slot):
+        if ITEMS[k][1]:
+            plane_copy(SHARED.index(k), slot).start()
+        core_copy(k, slot, core).start()
 
     def stage_2(k):
         for slot in range(3):
             first_arrival(k, slot).wait_recv()
         for slot in range(2):
             second_copy(k, slot).start()
-        core_copy(k, 0, core).start()
+        hand_on(k, 0)
 
     def stage_3(k):
         for slot in range(2):
             second_arrival(k, slot).wait_recv()
         onward_copy(k).start()
         for slot in range(2):
-            core_copy(k, 1 + slot, core).start()
+            hand_on(k, 1 + slot)
 
     def stage_4(k):
         onward_arrival(k).wait_recv()
-        core_copy(k, 3, core).start()
+        hand_on(k, 3)
+
+    def take_planes(n, slots):
+        for slot in slots:
+            plane_arrival(n, slot).wait_recv()
+            pass_copy(n, slot, core).start()
 
     def settle(k):
         for slot in range(4):
             core_copy(k, slot, 1 - core).wait_recv()
+
+    def settle_planes(n):
+        for slot in range(4):
+            pass_copy(n, slot, 1 - core).wait_recv()
 
     def row_copy(side, f, b):
         step = (1, -1)[side]
@@ -151,30 +190,32 @@
             f_send.at[2 * f + b], f_recv.at[2 * f + b], at_tm(tm - 1),
         )
 
-    def corner_copy(side):
+    def corner_copy(side, f):
         return remote(
-            cot.at[2 * side, pl.ds(0, 4)], cot.at[2 * side, pl.ds(6, 4)],
-            c_send.at[side], c_recv.at[side], at_tm(tm - 1),
-        )
-
-    def start_rows(side):
-        for f in range(3):
-            for b in range(2):
+            cot.at[2 * side, pl.ds(2 * f, 2)], cot.at[2 * side, pl.ds(6 + 2 * f, 2)],
+            c_send.at[side, f], c_recv.at[side, f], at_tm(tm - 1),
+        )
+
+    def start_rows(f):
+        for b in range(2):
+            for side in range(2):
                 row_copy(side, f, b).start()
 
-    def finish_rows(side):
-        for f in range(3):
+    def finish_rows(f):
+        for side in range(2):
             for b in range(2):
                 row_copy(side, f, b).wait_recv()
 
-        @pl.when(row == (0, 15)[side])
-        def _():
-            cot[2 * side, pl.ds(0, 6)] = jnp.zeros((6, 160, 512), cot.dtype)
-
-        corner_copy(side).start()
+            @pl.when(row == (0, 15)[side])
+            def _():
+                cot[2 * side, pl.ds(2 * f, 2)] = jnp.zeros((2, 160, 512), cot.dtype)
+
+            if f < 2:
+                corner_copy(side, f).start()
 
     def finish_corner(side):
-        corner_copy(side).wait_recv()
+        for f in range(2):
+            corner_copy(side, f).wait_recv()
 
         @pl.when(tm == 15)
         def _():
@@ -226,9 +267,8 @@
             square = square + each * (apart * apart)
         return mean, square
 
-    def matmul_chunk(k):
-        j = ORDER[k]
-        kr, kw = j // 3, j % 3
+    def matmul_chunk(kr, kw):
+        j = 3 * kr + kw
 
         def body(m, carry):
             total = None
@@ -241,7 +281,7 @@
                 total = part if total is None else total + part
             total = total.reshape(3, 160, 512)
             here = pl.ds(3 * m, 3)
-            if k < 3:
+            if kr == 1:
                 acc[kw, here] = total
             else:
                 acc[kw, here] = acc[kw, here] + total
@@ -269,7 +309,8 @@
     lax.fori_loop(1, 16, greet, 0)
 
     loads = [
-        pltpu.make_async_copy(wt_hbm.at[:, :, core], kern.at[:, :, px, py, core], load_sem.at[0])
+        pltpu.make_async_copy(wt_hbm.at[:, tap(k), core], piece(k, 0, core), load_sem.at[13 + k])
+        for k in range(6)
     ]
     for f in range(3):
         for b in range(2):
@@ -292,9 +333,25 @@
     for f in range(2):
         for b in range(2):
             frame_copy(f, b).start()
-    start_rows(1)
+    start_rows(0)
     for load in loads:
         load.wait()
+
+    chan_of = lax.broadcasted_iota(jnp.int32, (512, 128), 0)
+    group_of = lax.broadcasted_iota(jnp.int32, (512, 128), 1)
+    picks = (chan_of == group_of * per).astype(F32)
+    members = (chan_of // per == group_of).astype(F32)
+
+    def compact(value, chosen):
+        return jnp.dot(
+            value, chosen, precision=lax.Precision.HIGHEST, preferred_element_type=F32
+        )
+
+    def spread(value):
+        return lax.dot_general(
+            value, members, (((1,), (1,)), ((), ())),
+            precision=lax.Precision.HIGHEST, preferred_element_type=F32,
+        )
 
     def add_up(fn):
         rows = []
@@ -313,25 +370,22 @@
         return apart * apart
 
     own_square = group_total(add_up(deviation), per)
-    local[0, 0:2] = own_mean
-    local[0, 2:4] = own_square
-    local[0, 4:8] = jnp.zeros((4, 512), F32)
+    zeros = jnp.zeros((4, own_mean.shape[1]), F32)
+    local[0] = compact(jnp.concatenate([own_mean, own_square, zeros], axis=0), picks)
     exchange_start(0)
 
     def merge_rows():
         exchange_finish(0)
         mean, square = merge(0, float(local_count))
-        local[1, 0:2] = mean
-        local[1, 2:4] = square
-        local[1, 4:8] = jnp.zeros((4, 512), F32)
+        local[1] = jnp.concatenate([mean, square, jnp.zeros((4, 128), F32)], axis=0)
         exchange_start(1)
 
     def merge_all():
         exchange_finish(1)
         mean, square = merge(1, float(local_count) * 16)
         rstd = lax.rsqrt(square * (1.0 / count) + EPS)
-        moments[0:2] = mean
-        moments[2:4] = rstd
+        both = jnp.concatenate([mean, rstd, jnp.zeros((4, 128), F32)], axis=0)
+        moments[...] = spread(both)
 
     def prepare():
         def body(s, carry):
@@ -346,37 +400,56 @@
 
         lax.fori_loop(0, 6, body, 0)
 
-    for t in range(CHUNKS + 3):
-        if t < CHUNKS:
+    def work(k):
+        settle(k)
+        matmul_chunk(ITEMS[k][0], 2 * odd if ITEMS[k][1] else 1)
+
+    def work_planes(n):
+        settle_planes(n)
+        matmul_chunk(ITEMS[SHARED[n]][0], 2 - 2 * odd)
+
+    for t in range(10):
+        if t < 6:
             stage_2(t)
-        if t + 2 < CHUNKS:
+        if t + 2 < 6:
             stage_1(t + 2)
-        if t == 0:
-            start_rows(0)
-        if 0 <= t - 1 < CHUNKS:
+        if t < 2:
+            start_rows(t + 1)
+        if 0 <= t - 1 < 6:
             stage_3(t - 1)
-        if 0 <= t - 2 < CHUNKS:
+        if 0 <= t - 2 < 6:
             stage_4(t - 2)
+        for n in range(3):
+            late = t - SHARED[n] - 3
+            if 0 <= late < 3:
+                take_planes(n, ((0,), (1, 2), (3,))[late])
         if t == 2:
             merge_rows()
+            finish_rows(0)
+        elif t == 3:
+            finish_rows(1)
             finish_frames()
-        if t == 3:
-            finish_rows(1)
-        if t == 4:
+            work(0)
+        elif t == 4:
+            finish_rows(2)
             merge_all()
-            finish_rows(0)
-        if t == 5:
+            work(1)
+        elif t == 5:
             prepare()
-        k = t - 3
-        if k >= 0:
-            if k == 3:
-                finish_corner(1)
-            if k == 6:
-                finish_corner(0)
-            settle(k)
-            matmul_chunk(k)
-            if k == CHUNKS - 2:
-                fold_columns()
+        elif t == 6:
+            work_planes(0)
+            finish_corner(1)
+            work(2)
+        elif t == 7:
+            work(4)
+            finish_corner(0)
+            work(3)
+        elif t == 8:
+            work_planes(1)
+        elif t == 9:
+            work_planes(2)
+            fold_columns()
+            work(5)
 
     def terms(s, b):
         grad = acc[1, s] * scale[s]
@@ -385,14 +458,14 @@
 
     first = add_up(terms)
     second = add_up(lambda s, b: acc[1, s] * normed[s])
-    local[2, 0:4] = group_total(jnp.concatenate([first, second], axis=0), per)
-    local[2, 4:8] = jnp.zeros((4, 512), F32)
+    local[2] = compact(jnp.concatenate([first, second, zeros], axis=0), members)
     exchange_start(2)
     exchange_finish(2)
     local[3] = functools.reduce(jnp.add, [gathered[2, i] for i in range(16)])
     exchange_start(3)
     exchange_finish(3)
-    means = functools.reduce(jnp.add, [gathered[3, i] for i in range(16)]) * (1.0 / count)
+    totals = functools.reduce(jnp.add, [gathered[3, i] for i in range(16)])
+    means = spread(totals * (1.0 / count))
 
     stores = []
     for s in range(6):
@@ -404,7 +477,7 @@
         store.start()
         stores.append(store)
 
-    for k in range(CHUNKS):
+    for k in range(6):
         for slot in range(3):
             first_copy(k, slot).wait_send()
         for slot in range(2):
@@ -412,14 +485,19 @@
         onward_copy(k).wait_send()
         for slot in range(4):
             core_copy(k, slot, core).wait_send()
+    for n in range(3):
+        for slot in range(4):
+            plane_copy(n, slot).wait_send()
+            pass_copy(n, slot, core).wait_send()
     for f in range(3):
-        for b in range(2):
-            for side in range(2):
+        for side in range(2):
+            for b in range(2):
                 row_copy(side, f, b).wait_send()
             if f < 2:
+                corner_copy(side, f).wait_send()
+        if f < 2:
+            for b in range(2):
                 frame_copy(f, b).wait_send()
-    for side in range(2):
-        corner_copy(side).wait_send()
 
     def sent(k, carry):
         for e in range(4):
@@ -453,15 +531,16 @@
             pltpu.VMEM((6, width, chan), F32),
             pltpu.VMEM((6, width, chan), F32),
             pltpu.VMEM((6, width, chan), bf16),
-            pltpu.VMEM((4, 8, chan), F32),
-            pltpu.VMEM((4, 16, 8, chan), F32),
-            pltpu.VMEM((4, chan), F32),
-            dma((CHUNKS, 10)), dma((CHUNKS, 10)),
+            pltpu.VMEM((4, 8, 128), F32),
+            pltpu.VMEM((4, 16, 8, 128), F32),
+            pltpu.VMEM((8, chan), F32),
+            dma((6, 10)), dma((6, 10)),
+            dma((3, 8)), dma((3, 8)),
             dma((2, 6)), dma((2, 6)),
             dma((4,)), dma((4,)),
-            dma((2,)), dma((2,)),
+            dma((2, 2)), dma((2, 2)),
             dma((4, 16)), dma((4, 16)),
-            dma((13,)), dma((6,)),
+            dma((19,)), dma((6,)),
         ],
         compiler_params=pltpu.CompilerParams(
             collective_id=0, has_side_effects=True, vmem_limit_bytes=56 << 20

time: 141 us -> 112 us (0.79)
  Pallas kernels: 139 us -> 109 us
    pallas_call x1, Pallas kernels: 139 us -> 109 us  [shards(): pl.pallas_call(functools.partial(kernel, count), out_shape=jax.ShapeDtype...]
where the time goes in v2:
time: 112 us
  Pallas kernels  109 us (97%)
  local copies, waits for them, and re-layouts  2.26 us (2%)
    pallas_call x1, Pallas kernels, shards(): pl.pallas_call(functools.partial(kernel, count), out_shape=jax.ShapeDtype...  109 us
    unnamed x1, local copies, waits for them, and re-layouts  2.26 us

profile of v2, /device:TPU:1, one launch (start us, length us, event | category | flops | bytes accessed | tf_op | source)
XLA Modules:
  0.0 111.6 jit_solution(2544874114859293501)
XLA Ops:
  0.0 109.3 %conv_grad.1 = bf16[2,3,1,160,512]{4,3,2,1,0:T(8,128)(2,1)} custom-call(bf16[2,3,1,160,512]{4,3,2,1,0:T(8,128)(2,1)} %hid_hbm.1, bf16[2,3,1,160,512]{4,3,2,1,0:T(8,128)(2,1)} %cot_hbm.1, f32[1,512]{1,0:T(1,128)} %bitcast.6, f32[1,512]{1,0:T(1,128)} %bitcast.7, bf16[3,9,2,16,512]{4,3,2,1,0:T(8,128)(2,1)} %bitcast.5), custom_call_target="tpu_custom_call" | custom-call | tf_op jit(solution)/shard_map/conv_grad/pallas_call | solution.py:521
  109.4 2.3 %copy.7 = bf16[2,3,1,160,512]{4,3,2,1,0:T(8,128)(2,1)} copy(bf16[2,3,1,160,512]{4,3,2,1,0:T(8,128)(2,1)} %conv_grad.1) | data formatting | bytes 1966080

commit v3 on v2

--- a/solution.py
+++ b/solution.py
@@ -10,11 +10,15 @@
 GROUPS = 32
 MESH = pl.DeviceIdType.MESH
 F32 = jnp.float32
-ITEMS = (
-    (1, True, True), (1, False, True), (0, True, True),
-    (2, True, True), (0, False, True), (2, False, False),
+ITEMS = ((3, 5, True), (0, 2, False), (6, 8, True), (1, 7, True), (4, 4, False))
+SCHEDULE = (
+    "F", "A0", "A1", "A2", "A3", "A4", "E", "B0", "H00", "H01", "B1", "C0", "H10", "H11", "J",
+    "M", "B2", "C1", "D0", "H20", "H21", "N", "B3", "C2", "D1", "P0", "P1", "P2", "T00", "W00",
+    "P3", "W01", "I0", "B4", "C3", "D2", "P4", "T01", "P5", "I1", "T10", "T02", "V00", "V01",
+    "C4", "D3", "T11", "I2", "T20", "K1", "W10", "W11", "T12", "K0", "W20", "D4", "T21", "W21",
+    "V10", "V11", "T30", "T22", "W30", "W31", "T31", "V20", "V21", "T32", "X", "V30", "V31",
 )
-SHARED = tuple(i for i, item in enumerate(ITEMS) if item[1])
+SHARED = 4
 EPS = 1e-06
 
 
@@ -35,13 +39,14 @@
     count,
     hid_hbm, cot_hbm, gain_ref, shift_ref, wt_hbm, out_hbm,
     kern, cot, acc, hid, normed, scale, result, local, gathered, moments,
-    w_send, w_recv, z_send, z_recv, h_send, h_recv, f_send, f_recv, c_send, c_recv,
+    w_send, w_recv, z_send, z_recv, h_send, h_recv, f_send, f_recv, c_send, c_recv, v_send, v_recv,
     x_send, x_recv, load_sem, out_sem,
 ):
     tm, row = lax.axis_index("tm"), lax.axis_index("row")
     core = lax.rem(tm, 2)
     px, py = row // 4, lax.rem(row, 4)
     way = 1 - 2 * core
+    x_way = jnp.where(py == 3, -1, jnp.where(py == 0, 1, way))
     odd = lax.rem(tm // 2, 2)
     per = gain_ref.shape[1] // GROUPS
     local_count = 3 * 160 * per
@@ -67,10 +72,12 @@
         )
 
     def tap(k):
-        return 3 * ITEMS[k][0] + (2 * odd if ITEMS[k][1] else 1)
+        even, other, _ = ITEMS[k]
+        return even + odd * (other - even)
 
     def other_tap(n):
-        return 3 * ITEMS[SHARED[n]][0] + 2 - 2 * odd
+        even, other, _ = ITEMS[n]
+        return other + odd * (even - other)
 
     def along(k, step):
         return at_xy(px, py + step) if ITEMS[k][2] else at_xy(px + step, py)
@@ -111,8 +118,9 @@
         return remote(mine, mine, w_send.at[k, 3 + slot], w_recv.at[k, 3 + slot], across(k, step))
 
     def onward_copy(k):
-        mine = block(k, -way, core)
-        return remote(mine, mine, w_send.at[k, 5], w_recv.at[k, 5], across(k, way))
+        step = x_way if ITEMS[k][2] else way
+        mine = block(k, -step, core)
+        return remote(mine, mine, w_send.at[k, 5], w_recv.at[k, 5], across(k, step))
 
     def onward_arrival(k):
         mine = block(k, 2, core)
@@ -124,26 +132,37 @@
         mine = block(k, STEPS[slot], half)
         return remote(mine, mine, w_send.at[k, 6 + slot], w_recv.at[k, 6 + slot], partner)
 
-    def plane_copy(n, slot):
-        mine = block(SHARED[n], STEPS[slot], core)
-        step = 1 if n == 0 else way
-        return remote(mine, mine, z_send.at[n, slot], z_recv.at[n, slot], at_tm(tm + 2 * step))
-
-    def plane_arrival(n, slot):
-        mine = block(SHARED[n], STEPS[slot], core, other_tap(n))
-        return remote(mine, mine, z_send.at[n, slot], z_recv.at[n, slot], partner)
+    def share(n, slot, end, chosen=None):
+        k = n
+        chosen = tap(k) if chosen is None else chosen
+        there = pl.ds(2 * end, 2)
+        if ITEMS[k][2]:
+            return kern.at[:, chosen, wrap(px + STEPS[slot], 4), there, core]
+        return kern.at[:, chosen, there, wrap(py + STEPS[slot], 4), core]
+
+    def plane_copy(n, slot, end):
+        mine = share(n, slot, end)
+        return remote(
+            mine, mine, z_send.at[n, slot, end], z_recv.at[n, slot, end],
+            at_tm(tm + (2, -2)[end]),
+        )
+
+    def plane_arrival(n, slot, end):
+        mine = share(n, slot, end, other_tap(n))
+        return remote(mine, mine, z_send.at[n, slot, end], z_recv.at[n, slot, end], partner)
 
     def pass_copy(n, slot, half):
-        mine = block(SHARED[n], STEPS[slot], half, other_tap(n))
-        return remote(mine, mine, z_send.at[n, 4 + slot], z_recv.at[n, 4 + slot], partner)
+        mine = block(n, STEPS[slot], half, other_tap(n))
+        return remote(mine, mine, z_send.at[n, slot, 2], z_recv.at[n, slot, 2], partner)
 
     def stage_1(k):
         for slot in (2, 0, 1):
             first_copy(k, slot).start()
 
     def hand_on(k, slot):
-        if ITEMS[k][1]:
-            plane_copy(SHARED.index(k), slot).start()
+        if k < SHARED:
+            for end in range(2):
+                plane_copy(k, slot, end).start()
         core_copy(k, slot, core).start()
 
     def stage_2(k):
@@ -164,9 +183,10 @@
         onward_arrival(k).wait_recv()
         hand_on(k, 3)
 
-    def take_planes(n, slots):
-        for slot in slots:
-            plane_arrival(n, slot).wait_recv()
+    def take_planes(n, part):
+        for slot in ((0,), (1, 2), (3,))[part]:
+            for end in range(2):
+                plane_arrival(n, slot, end).wait_recv()
             pass_copy(n, slot, core).start()
 
     def settle(k):
@@ -193,13 +213,18 @@
     def corner_copy(side, f):
         return remote(
             cot.at[2 * side, pl.ds(2 * f, 2)], cot.at[2 * side, pl.ds(6 + 2 * f, 2)],
-            c_send.at[side, f], c_recv.at[side, f], at_tm(tm - 1),
-        )
-
-    def start_rows(f):
-        for b in range(2):
-            for side in range(2):
-                row_copy(side, f, b).start()
+            c_send.at[side, f], c_recv.at[side, f], partner,
+        )
+
+    def wing_copy(side):
+        return remote(
+            cot.at[1, pl.ds(6, 4)], cot.at[2 * side, pl.ds(6, 4)],
+            v_send.at[side], v_recv.at[side], at_row(row + (1, -1)[side]),
+        )
+
+    def start_rows(f, b):
+        for side in range(2):
+            row_copy(side, f, b).start()
 
     def finish_rows(f):
         for side in range(2):
@@ -211,13 +236,22 @@
                 cot[2 * side, pl.ds(2 * f, 2)] = jnp.zeros((2, 160, 512), cot.dtype)
 
             if f < 2:
-                corner_copy(side, f).start()
+
+                @pl.when(core == 1)
+                def _():
+                    corner_copy(side, f).start()
 
     def finish_corner(side):
-        for f in range(2):
-            corner_copy(side, f).wait_recv()
-
-        @pl.when(tm == 15)
+        @pl.when(core == 0)
+        def _():
+            for f in range(2):
+                corner_copy(side, f).wait_recv()
+
+        @pl.when(core == 1)
+        def _():
+            wing_copy(side).wait_recv()
+
+        @pl.when(row == (0, 15)[side])
         def _():
             cot[2 * side, pl.ds(6, 4)] = jnp.zeros((4, 160, 512), cot.dtype)
 
@@ -229,6 +263,11 @@
         @pl.when(tm == 15)
         def _():
             cot[1, pl.ds(6, 4)] = jnp.zeros((4, 160, 512), cot.dtype)
+
+        @pl.when(core == 1)
+        def _():
+            for side in range(2):
+                wing_copy(side).start()
 
     def exchange_copy(e, k):
         if e % 2 == 0:
@@ -267,27 +306,20 @@
             square = square + each * (apart * apart)
         return mean, square
 
-    def matmul_chunk(kr, kw):
-        j = 3 * kr + kw
-
-        def body(m, carry):
-            total = None
-            for kt in range(3):
-                lhs = cot[2 - kr, pl.ds(2 * (2 - kt) + 3 * m, 3)].reshape(480, 512)
-                rhs = kern[kt, j].reshape(512, 512)
-                part = lax.dot_general(
-                    lhs, rhs, (((1,), (1,)), ((), ())), preferred_element_type=F32
-                )
-                total = part if total is None else total + part
-            total = total.reshape(3, 160, 512)
-            here = pl.ds(3 * m, 3)
-            if kr == 1:
-                acc[kw, here] = total
-            else:
-                acc[kw, here] = acc[kw, here] + total
-            return carry
-
-        lax.fori_loop(0, 2, body, 0)
+    def product(m, kr, kw):
+        total = None
+        for kt in range(3):
+            lhs = cot[2 - kr, pl.ds(2 * (2 - kt) + 3 * m, 3)].reshape(480, 512)
+            rhs = kern[kt, 3 * kr + kw].reshape(512, 512)
+            part = lax.dot_general(
+                lhs, rhs, (((1,), (1,)), ((), ())), preferred_element_type=F32
+            )
+            total = part if total is None else total + part
+        return total.reshape(3, 160, 512)
+
+    def matmul_half(m, kr, kw):
+        here = pl.ds(3 * m, 3)
+        acc[kw, here] = acc[kw, here] + product(m, kr, kw)
 
     def fold_columns():
         def body(s, carry):
@@ -310,7 +342,7 @@
 
     loads = [
         pltpu.make_async_copy(wt_hbm.at[:, tap(k), core], piece(k, 0, core), load_sem.at[13 + k])
-        for k in range(6)
+        for k in range(5)
     ]
     for f in range(3):
         for b in range(2):
@@ -326,15 +358,9 @@
             )
     for load in loads:
         load.start()
-
-    pl.semaphore_wait(barrier, 30)
-    stage_1(0)
-    stage_1(1)
-    for f in range(2):
-        for b in range(2):
-            frame_copy(f, b).start()
-    start_rows(0)
-    for load in loads:
+    acc[...] = jnp.zeros_like(acc)
+
+    for load in loads[5:11]:
         load.wait()
 
     chan_of = lax.broadcasted_iota(jnp.int32, (512, 128), 0)
@@ -372,8 +398,9 @@
     own_square = group_total(add_up(deviation), per)
     zeros = jnp.zeros((4, own_mean.shape[1]), F32)
     local[0] = compact(jnp.concatenate([own_mean, own_square, zeros], axis=0), picks)
-    exchange_start(0)
-
+    pl.semaphore_wait(barrier, 30)
+    for load in loads[:5] + loads[11:]:
+        load.wait()
     def merge_rows():
         exchange_finish(0)
         mean, square = merge(0, float(local_count))
@@ -387,97 +414,59 @@
         both = jnp.concatenate([mean, rstd, jnp.zeros((4, 128), F32)], axis=0)
         moments[...] = spread(both)
 
-    def prepare():
-        def body(s, carry):
-            b = lax.rem(s, 2)
-            mean, rstd = moments[pl.ds(b, 1)], moments[pl.ds(2 + b, 1)]
-            unit = (hid[s].astype(F32) - mean) * rstd
-            pre = unit * gain_ref[...] + shift_ref[...]
-            sig = 1.0 / (1.0 + jnp.exp(-pre))
-            normed[s] = unit
-            scale[s] = sig * (1.0 + pre * (1.0 - sig)) * gain_ref[...]
-            return carry
-
-        lax.fori_loop(0, 6, body, 0)
-
-    def work(k):
-        settle(k)
-        matmul_chunk(ITEMS[k][0], 2 * odd if ITEMS[k][1] else 1)
-
-    def work_planes(n):
-        settle_planes(n)
-        matmul_chunk(ITEMS[SHARED[n]][0], 2 - 2 * odd)
-
-    for t in range(10):
-        if t < 6:
-            stage_2(t)
-        if t + 2 < 6:
-            stage_1(t + 2)
-        if t < 2:
-            start_rows(t + 1)
-        if 0 <= t - 1 < 6:
-            stage_3(t - 1)
-        if 0 <= t - 2 < 6:
-            stage_4(t - 2)
-        for n in range(3):
-            late = t - SHARED[n] - 3
-            if 0 <= late < 3:
-                take_planes(n, ((0,), (1, 2), (3,))[late])
-        if t == 2:
-            merge_rows()
-            finish_rows(0)
-        elif t == 3:
-            finish_rows(1)
-            finish_frames()
-            work(0)
-        elif t == 4:
-            finish_rows(2)
-            merge_all()
-            work(1)
-        elif t == 5:
-            prepare()
-        elif t == 6:
-            work_planes(0)
-            finish_corner(1)
-            work(2)
-        elif t == 7:
-            work(4)
-            finish_corner(0)
-            work(3)
-        elif t == 8:
-            work_planes(1)
-        elif t == 9:
-            work_planes(2)
-            fold_columns()
-            work(5)
-
-    def terms(s, b):
-        grad = acc[1, s] * scale[s]
-        acc[1, s] = grad
-        return grad
-
-    first = add_up(terms)
-    second = add_up(lambda s, b: acc[1, s] * normed[s])
+    def prepare(s):
+        b = s % 2
+        mean, rstd = moments[b : b + 1], moments[2 + b : 3 + b]
+        unit = (hid[s].astype(F32) - mean) * rstd
+        pre = unit * gain_ref[...] + shift_ref[...]
+        sig = 1.0 / (1.0 + jnp.exp(-pre))
+        normed[s] = unit
+        scale[s] = sig * (1.0 + pre * (1.0 - sig)) * gain_ref[...]
+
+    def start_frames():
+        for f in range(2):
+            for b in range(2):
+                frame_copy(f, b).start()
+
+    def start_stats():
+        exchange_start(0)
+
+    def work(k, m):
+        if m == 0:
+            settle(k)
+        matmul_half(m, tap(k) // 3, lax.rem(tap(k), 3))
+
+    def work_planes(n, m):
+        if m == 0:
+            settle_planes(n)
+        matmul_half(m, other_tap(n) // 3, lax.rem(other_tap(n), 3))
+
+    steps = {
+        "A": stage_1, "B": stage_2, "C": stage_3, "D": stage_4, "T": take_planes,
+        "F": start_frames, "H": start_rows, "I": finish_rows, "J": finish_frames,
+        "K": finish_corner, "E": start_stats, "M": merge_rows, "N": merge_all, "P": prepare,
+        "W": work, "V": work_planes, "X": fold_columns,
+    }
+    for step in SCHEDULE:
+        steps[step[0]](*(int(digit) for digit in step[1:]))
+    settle(4)
+
+    sums = [[None, None], [None, None]]
+    for m in range(2):
+        whole = acc[1, 3 * m : 3 * m + 3] + product(m, 1, 1)
+        for i in range(3):
+            s = 3 * m + i
+            grad = whole[i] * scale[s]
+            acc[1, s] = grad
+            for kind, value in enumerate((grad, grad * normed[s])):
+                part = jnp.sum(value, axis=0, keepdims=True)
+                held = sums[kind][s % 2]
+                sums[kind][s % 2] = part if held is None else held + part
+    first, second = (jnp.concatenate(pair, axis=0) for pair in sums)
     local[2] = compact(jnp.concatenate([first, second, zeros], axis=0), members)
     exchange_start(2)
-    exchange_finish(2)
-    local[3] = functools.reduce(jnp.add, [gathered[2, i] for i in range(16)])
-    exchange_start(3)
-    exchange_finish(3)
-    totals = functools.reduce(jnp.add, [gathered[3, i] for i in range(16)])
-    means = spread(totals * (1.0 / count))
-
-    stores = []
-    for s in range(6):
-        f, b = s // 2, s % 2
-        rstd = moments[2 + b : 3 + b]
-        value = rstd * (acc[1, s] - means[b : b + 1] - normed[s] * means[2 + b : 3 + b])
-        result[s] = value.astype(result.dtype)
-        store = pltpu.make_async_copy(result.at[s], out_hbm.at[b, f, 0], out_sem.at[s])
-        store.start()
-        stores.append(store)
-
-    for k in range(6):
+
+    for k in range(5):
         for slot in range(3):
             first_copy(k, slot).wait_send()
         for slot in range(2):
@@ -485,19 +474,29 @@
         onward_copy(k).wait_send()
         for slot in range(4):
             core_copy(k, slot, core).wait_send()
-    for n in range(3):
+    for n in range(SHARED):
         for slot in range(4):
-            plane_copy(n, slot).wait_send()
+            for end in range(2):
+                plane_copy(n, slot, end).wait_send()
             pass_copy(n, slot, core).wait_send()
+    @pl.when(core == 1)
+    def _():
+        for side in range(2):
+            wing_copy(side).wait_send()
+            for f in range(2):
+                corner_copy(side, f).wait_send()
+
     for f in range(3):
         for side in range(2):
             for b in range(2):
                 row_copy(side, f, b).wait_send()
-            if f < 2:
-                corner_copy(side, f).wait_send()
         if f < 2:
             for b in range(2):
                 frame_copy(f, b).wait_send()
+
+    exchange_finish(2)
+    local[3] = functools.reduce(jnp.add, [gathered[2, i] for i in range(16)])
+    exchange_start(3)
 
     def sent(k, carry):
         for e in range(4):
@@ -505,6 +504,21 @@
         return carry
 
     lax.fori_loop(1, 16, sent, 0)
+    exchange_finish(3)
+    totals = functools.reduce(jnp.add, [gathered[3, i] for i in range(16)])
+    means = spread(totals * (1.0 / count))
+
+    stores = []
+    for s in range(6):
+        f, b = s // 2, s % 2
+        rstd = moments[2 + b : 3 + b]
+        low, slope = rstd * means[b : b + 1], rstd * means[2 + b : 3 + b]
+        value = rstd * acc[1, s] - low - normed[s] * slope
+        result[s] = value.astype(result.dtype)
+        store = pltpu.make_async_copy(result.at[s], out_hbm.at[b, f, 0], out_sem.at[s])
+        store.start()
+        stores.append(store)
+
     for store in stores:
         store.wait()
 
@@ -534,13 +548,14 @@
             pltpu.VMEM((4, 8, 128), F32),
             pltpu.VMEM((4, 16, 8, 128), F32),
             pltpu.VMEM((8, chan), F32),
-            dma((6, 10)), dma((6, 10)),
-            dma((3, 8)), dma((3, 8)),
+            dma((5, 10)), dma((5, 10)),
+            dma((4, 4, 3)), dma((4, 4, 3)),
             dma((2, 6)), dma((2, 6)),
             dma((4,)), dma((4,)),
             dma((2, 2)), dma((2, 2)),
+            dma((2,)), dma((2,)),
             dma((4, 16)), dma((4, 16)),
-            dma((19,)), dma((6,)),
+            dma((18,)), dma((6,)),
         ],
         compiler_params=pltpu.CompilerParams(
             collective_id=0, has_side_effects=True, vmem_limit_bytes=56 << 20

time: 112 us -> 96.6 us (0.86)
  Pallas kernels: 109 us -> 94.2 us
    pallas_call x1, Pallas kernels: 109 us -> 94.2 us  [shards(): pl.pallas_call(functools.partial(kernel, count), out_shape=jax.ShapeDtype...]
where the time goes in v3:
time: 96.6 us; the launch traced here: 96.4 us
  Pallas kernels  94.2 us (98%)
  local copies, waits for them, and re-layouts  2.26 us (2%)
    pallas_call x1, Pallas kernels, shards(): pl.pallas_call(functools.partial(kernel, count), out_shape=jax.ShapeDtype...  94.2 us
    unnamed x1, local copies, waits for them, and re-layouts  2.26 us

profile of v3, /device:TPU:1, one launch (start us, length us, event | category | flops | bytes accessed | tf_op | source)
XLA Modules:
  0.0 96.4 jit_solution(7349698494192839286)
XLA Ops:
  0.0 94.2 %conv_grad.1 = bf16[2,3,1,160,512]{4,3,2,1,0:T(8,128)(2,1)} custom-call(bf16[2,3,1,160,512]{4,3,2,1,0:T(8,128)(2,1)} %hid_hbm.1, bf16[2,3,1,160,512]{4,3,2,1,0:T(8,128)(2,1)} %cot_hbm.1, f32[1,512]{1,0:T(1,128)} %bitcast.6, f32[1,512]{1,0:T(1,128)} %bitcast.7, bf16[3,9,2,16,512]{4,3,2,1,0:T(8,128)(2,1)} %bitcast.5), custom_call_target="tpu_custom_call" | custom-call | tf_op jit(solution)/shard_map/conv_grad/pallas_call | solution.py:535
  94.2 2.3 %copy.7 = bf16[2,3,1,160,512]{4,3,2,1,0:T(8,128)(2,1)} copy(bf16[2,3,1,160,512]{4,3,2,1,0:T(8,128)(2,1)} %conv_grad.1) | data formatting | bytes 1966080

commit v4 on v3

--- a/solution.py
+++ b/solution.py
@@ -12,11 +12,12 @@
 F32 = jnp.float32
 ITEMS = ((3, 5, True), (0, 2, False), (6, 8, True), (1, 7, True), (4, 4, False))
 SCHEDULE = (
-    "F", "A0", "A1", "A2", "A3", "A4", "E", "B0", "H00", "H01", "B1", "C0", "H10", "H11", "J",
-    "M", "B2", "C1", "D0", "H20", "H21", "N", "B3", "C2", "D1", "P0", "P1", "P2", "T00", "W00",
-    "P3", "W01", "I0", "B4", "C3", "D2", "P4", "T01", "P5", "I1", "T10", "T02", "V00", "V01",
-    "C4", "D3", "T11", "I2", "T20", "K1", "W10", "W11", "T12", "K0", "W20", "D4", "T21", "W21",
-    "V10", "V11", "T30", "T22", "W30", "W31", "T31", "V20", "V21", "T32", "X", "V30", "V31",
+    "F", "A0", "A1", "A2", "A3", "A4", "E", "B0", "H00", "B1", "C0", "H01", "H10", "J", "M",
+    "B2", "C1", "D0", "H11", "H20", "N", "B3", "C2", "D1", "H21", "P0", "P1", "P2", "T00",
+    "W00", "P3", "W01", "I0", "I1", "B4", "C3", "D2", "P4", "T01", "P5", "T10", "T02", "V00",
+    "V01", "C4", "D3", "T11", "I2", "K1", "W10", "W11", "T20", "T12", "K0", "W20", "W21", "D4",
+    "T30", "T21", "V10", "T22", "V11", "W30", "T31", "W31", "V20", "T32", "V21", "X", "V30",
+    "V31",
 )
 SHARED = 4
 EPS = 1e-06

time: 96.6 us -> 93.8 us (0.971)
  Pallas kernels: 94.2 us -> 91.4 us
    pallas_call x1, Pallas kernels: 94.2 us -> 91.4 us  [shards(): pl.pallas_call(functools.partial(kernel, count), out_shape=jax.ShapeDtype...]
where the time goes in v4:
time: 93.8 us; the launch traced here: 93.6 us
  Pallas kernels  91.4 us (97%)
  local copies, waits for them, and re-layouts  2.26 us (2%)
    pallas_call x1, Pallas kernels, shards(): pl.pallas_call(functools.partial(kernel, count), out_shape=jax.ShapeDtype...  91.4 us
    unnamed x1, local copies, waits for them, and re-layouts  2.26 us

profile of v4, /device:TPU:1, one launch (start us, length us, event | category | flops | bytes accessed | tf_op | source)
XLA Modules:
  0.0 93.6 jit_solution(16403876576740350266)
XLA Ops:
  0.0 91.4 %conv_grad.1 = bf16[2,3,1,160,512]{4,3,2,1,0:T(8,128)(2,1)} custom-call(bf16[2,3,1,160,512]{4,3,2,1,0:T(8,128)(2,1)} %hid_hbm.1, bf16[2,3,1,160,512]{4,3,2,1,0:T(8,128)(2,1)} %cot_hbm.1, f32[1,512]{1,0:T(1,128)} %bitcast.6, f32[1,512]{1,0:T(1,128)} %bitcast.7, bf16[3,9,2,16,512]{4,3,2,1,0:T(8,128)(2,1)} %bitcast.5), custom_call_target="tpu_custom_call" | custom-call | tf_op jit(solution)/shard_map/conv_grad/pallas_call | solution.py:536
  91.4 2.3 %copy.7 = bf16[2,3,1,160,512]{4,3,2,1,0:T(8,128)(2,1)} copy(bf16[2,3,1,160,512]{4,3,2,1,0:T(8,128)(2,1)} %conv_grad.1) | data formatting | bytes 1966080

commit v5 on v3

--- a/solution.py
+++ b/solution.py
@@ -12,11 +12,11 @@
 F32 = jnp.float32
 ITEMS = ((3, 5, True), (0, 2, False), (6, 8, True), (1, 7, True), (4, 4, False))
 SCHEDULE = (
-    "F", "A0", "A1", "A2", "A3", "A4", "E", "B0", "H00", "H01", "B1", "C0", "H10", "H11", "J",
-    "M", "B2", "C1", "D0", "H20", "H21", "N", "B3", "C2", "D1", "P0", "P1", "P2", "T00", "W00",
-    "P3", "W01", "I0", "B4", "C3", "D2", "P4", "T01", "P5", "I1", "T10", "T02", "V00", "V01",
-    "C4", "D3", "T11", "I2", "T20", "K1", "W10", "W11", "T12", "K0", "W20", "D4", "T21", "W21",
-    "V10", "V11", "T30", "T22", "W30", "W31", "T31", "V20", "V21", "T32", "X", "V30", "V31",
+    "F", "A0", "A1", "A2", "A3", "A4", "E", "B0", "H00", "B1", "C0", "H01", "H10", "M", "B2",
+    "C1", "D0", "H11", "H20", "J", "N", "B3", "C2", "D1", "H21", "P0", "P1", "P2", "T00", "W00",
+    "P3", "W01", "I0", "I1", "B4", "C3", "D2", "P4", "T01", "P5", "T10", "T02", "V00", "V01",
+    "C4", "D3", "T11", "I2", "K1", "W10", "W11", "T20", "T12", "K0", "W20", "W21", "D4", "T30",
+    "T21", "V10", "T22", "V11", "W30", "T31", "W31", "V20", "T32", "V21", "X", "V30", "V31",
 )
 SHARED = 4
 EPS = 1e-06

time: 96.6 us -> 96 us (level)
  no operation moved by 1% of the time
where the time goes in v5:
time: 96 us; the launch traced here: 95.8 us
  Pallas kernels  93.6 us (98%)
  local copies, waits for them, and re-layouts  2.26 us (2%)
    pallas_call x1, Pallas kernels, shards(): pl.pallas_call(functools.partial(kernel, count), out_shape=jax.ShapeDtype...  93.6 us
    unnamed x1, local copies, waits for them, and re-layouts  2.26 us

profile of v5, /device:TPU:1, one launch (start us, length us, event | category | flops | bytes accessed | tf_op | source)
XLA Modules:
  0.0 95.8 jit_solution(10879387503379798652)
XLA Ops:
  0.0 93.6 %conv_grad.1 = bf16[2,3,1,160,512]{4,3,2,1,0:T(8,128)(2,1)} custom-call(bf16[2,3,1,160,512]{4,3,2,1,0:T(8,128)(2,1)} %hid_hbm.1, bf16[2,3,1,160,512]{4,3,2,1,0:T(8,128)(2,1)} %cot_hbm.1, f32[1,512]{1,0:T(1,128)} %bitcast.6, f32[1,512]{1,0:T(1,128)} %bitcast.7, bf16[3,9,2,16,512]{4,3,2,1,0:T(8,128)(2,1)} %bitcast.5), custom_call_target="tpu_custom_call" | custom-call | tf_op jit(solution)/shard_map/conv_grad/pallas_call | solution.py:535
  93.6 2.3 %copy.7 = bf16[2,3,1,160,512]{4,3,2,1,0:T(8,128)(2,1)} copy(bf16[2,3,1,160,512]{4,3,2,1,0:T(8,128)(2,1)} %conv_grad.1) | data formatting | bytes 1966080
